TPU v7x, 512 devices: a whole 4x4x16 slice. The times are simulated.
512 devices in a mesh: dp: 16 (over x, y), tile: 32 (over z, core).
Axes of the slice: x: 4, y: 4, z: 16, core: 2. Of those that a mesh axis runs over, the one named last changes fastest.
Arguments:
- tiles: bfloat16 [524288, 1536], P(('dp', 'tile')), may hold values from -6 to 6
- slide_of_tile: int32 [16, 32768], P('dp', 'tile'), may hold values from 0 to 15, never falling along the last dimension, each value on 1 to 8192 neighbouring positions
- labels: int32 [16, 16], P('dp'), may hold values from 0 to 1
- attn_v: bfloat16 [1536, 512], replicated, may hold values from -0.15625 to 0.15625
- attn_u: bfloat16 [1536, 512], replicated, may hold values from -0.15625 to 0.15625
- score_w: bfloat16 [512, 8], replicated, may hold values from -200 to 200
- head_w1: bfloat16 [1536, 512], P('tile'), may hold values from -0.15625 to 0.15625
- head_w2: bfloat16 [512], replicated, may hold values from -0.25 to 0.25
Outputs:
- grad_w1: float32 [1536, 512], P('tile')
- grad_score: float32 [512, 8], replicated
- grad_w2: float32 [512], replicated
- mean_loss: float32 [], replicated
Inputs may be any that keep to these rules, and one draw needn't show every extreme that they name: In each row of slide_of_tile the slide numbers never fall; every slide 0 to 15 holds 1 to 8192 tiles, and one slide of each row holds exactly 8192.
All inputs are finite; a program needn't handle non-finite values.
Results may differ from a plain program's by a relative error of at most 0.0055.
The roundings to bfloat16 on the way count: a program that leaves them out, or rounds other values in their place, can miss the bound.
Values may be sent and summed in bfloat16 or wider, within the bound.
A program may use at most 64 MiB of HBM per device.

v0:
```python
import jax
import jax.numpy as jnp
from jax import lax
from jax.sharding import PartitionSpec as P

highest = lax.Precision.HIGHEST


def gelu_slope(values):
    return (
        0.5 * (1.0 + lax.erf(values * 0.7071067811865476))
        + values * jnp.exp(-0.5 * values * values) * 0.3989422804014327
    )


def spread(member, table):
    return jnp.sum(jnp.where(member[:, :, None], table[None, :, :], 0.0), axis=1)


def pool_terms(tiles, member, scores, shift):
    row_count, feature_count = tiles.shape
    head_count = scores.shape[1]
    expo = jnp.exp(scores - spread(member, shift))
    weights = jnp.where(member[:, :, None], expo[:, None, :], 0.0)
    totals = jnp.sum(weights, axis=0)
    upper = lax.optimization_barrier(weights.astype(jnp.bfloat16))
    lower = (weights - upper.astype(jnp.float32)).astype(jnp.bfloat16)
    split_rows = tiles.reshape(row_count, head_count, feature_count // head_count)
    pooled = jnp.einsum("isk,ikd->skd", upper, split_rows, preferred_element_type=jnp.float32)
    pooled = pooled + jnp.einsum(
        "isk,ikd->skd", lower, split_rows, preferred_element_type=jnp.float32
    )
    return (totals, pooled)


def body(tiles, slide_of_tile, labels, attn_v, attn_u, score_w, head_w1, head_w2):
    row_count, feature_count = tiles.shape
    slide_count = labels.shape[1]
    head_count = score_w.shape[1]
    head_part = feature_count // head_count
    segment = slide_of_tile[0]
    member = segment[:, None] == jnp.arange(slide_count, dtype=jnp.int32)[None, :]
    tanh_part = jnp.tanh(jnp.dot(tiles, attn_v, preferred_element_type=jnp.float32))
    gate_part = jax.nn.sigmoid(jnp.dot(tiles, attn_u, preferred_element_type=jnp.float32))
    gated = (tanh_part * gate_part).astype(jnp.bfloat16)
    scores = jnp.dot(gated, score_w, preferred_element_type=jnp.float32)
    local_max = jnp.max(jnp.where(member[:, :, None], scores[:, None, :], -jnp.inf), axis=0)
    global_max = lax.pmax(local_max, "tile")
    totals, pooled = pool_terms(tiles, member, scores, global_max)
    totals, pooled = lax.psum((totals, pooled), "tile")
    pooled = pooled / totals[:, :, None]
    flat_pool = pooled.reshape(slide_count, feature_count)
    root_mean = jnp.sqrt(jnp.mean(flat_pool * flat_pool, axis=1, keepdims=True) + 1e-05)
    normed = flat_pool / root_mean
    normed_low = normed.astype(jnp.bfloat16)
    width_rows = head_w1.shape[0]
    own_index = lax.axis_index("tile")
    normed_own = lax.dynamic_slice_in_dim(normed_low, own_index * width_rows, width_rows, 1)
    whole_w1 = lax.all_gather(head_w1, "tile", axis=0, tiled=True)
    pre_act = jnp.dot(normed_low, whole_w1, preferred_element_type=jnp.float32)
    hidden = jax.nn.gelu(pre_act, approximate=False)
    w2_float = head_w2.astype(jnp.float32)
    logits = jnp.dot(hidden, w2_float, precision=highest)
    target = labels[0].astype(jnp.float32)
    loss_terms = jax.nn.softplus(logits) - target * logits
    logit_grad = jax.nn.sigmoid(logits) - target
    w2_part = jnp.dot(logit_grad, hidden, precision=highest)
    pre_grad = logit_grad[:, None] * w2_float[None, :] * gelu_slope(pre_act)
    rows_part = jnp.dot(normed_own.astype(jnp.float32).T, pre_grad, precision=highest)
    grad_rows, grad_w2, loss_total = lax.psum((rows_part, w2_part, jnp.sum(loss_terms)), "dp")
    norm_grad = jnp.dot(pre_grad, whole_w1.astype(jnp.float32).T, precision=highest)
    flat_grad = (
        norm_grad - normed * jnp.mean(norm_grad * normed, axis=1, keepdims=True)
    ) / root_mean
    pool_grad = flat_grad.reshape(slide_count, head_count, head_part)
    inner_dot = jnp.sum(pooled * pool_grad, axis=2)
    onehot = member.astype(jnp.float32)
    tile_grad = jnp.dot(onehot, flat_grad, precision=highest)
    projected = jnp.sum(
        (tiles.astype(jnp.float32) * tile_grad).reshape(row_count, head_count, head_part), axis=2
    )
    softmax_w = jnp.exp(scores - spread(member, global_max)) / spread(member, totals)
    score_delta = softmax_w * (projected - spread(member, inner_dot))
    score_part = jnp.dot(gated.astype(jnp.float32).T, score_delta, precision=highest)
    grad_score = lax.psum(score_part, ("dp", "tile"))
    mean_loss = loss_total / (slide_count * lax.axis_size("dp"))
    return (grad_rows, grad_score, grad_w2, mean_loss)


def solution(mesh):
    return jax.shard_map(
        body,
        mesh=mesh,
        in_specs=(
            P(("dp", "tile"), None),
            P("dp", "tile"),
            P("dp", None),
            P(),
            P(),
            P(),
            P("tile", None),
            P(),
        ),
        out_specs=(P("tile", None), P(), P(), P()),
        check_vma=False,
    )
```

profile of v0, /device:TPU:1, one launch (start us, length us, event | category | flops | bytes accessed | tf_op | source)
XLA Modules:
  0.0 514.1 jit_solution(13148691613725231152)
XLA Ops:
  7.2 0.0 copy-start
  7.2 0.0 all-reduce.4.cloned.1.call-start
  7.2 0.8 iota_compare_fusion
  8.0 4.6 copy.14
  12.7 0.0 copy-done
  12.7 0.0 copy-start.2
  12.7 0.0 copy-start.7
  12.7 3.8 fusion.37
  16.5 0.0 copy-done.2
  16.5 0.0 copy-done.7
  16.5 0.0 copy-start.4
  16.6 2.3 multiply_convert_fusion
  18.9 0.0 copy-done.4
  18.9 0.4 fusion.38
  19.2 0.1 select_reduce_fusion.4
  19.4 53.3 %pmax.7 = f32[16,8]{0,1:T(8,128)S(1)} all-reduce(f32[16,8]{0,1:T(8,128)S(1)} %select_reduce_fusion.4), channel_id=1, replica_groups=mesh['dp'=16,'tile'=32] {'tile'}, use_global_device_ids=true, to_apply=%region_1.2 | all-reduce | flops 128 | bytes 1024 | tf_op jit(solution)/shard_map/pmax | solution.py:48
  72.7 0.0 copy-start.1
  72.7 0.2 select_reduce_fusion.3
  72.9 3.0 fusion.39
  75.9 0.0 copy-done.1
  75.9 0.0 copy-start.5
  75.9 1.6 fusion
  77.5 0.0 copy-start.6
  77.5 0.0 all-reduce.4.cloned.1.call-update
  77.5 0.0 all-gather.2.cloned.1.call-start
  77.6 0.7 all-gather.2.cloned.1.call-update
  78.3 0.0 all-reduce.6.cloned.1.call-start
  78.3 0.0 copy-done.5
  78.4 0.1 select_reduce_fusion
  78.5 48.1 %psum.43 = f32[16,8]{0,1:T(8,128)S(1)} all-reduce(f32[16,8]{0,1:T(8,128)S(1)} %select_reduce_fusion), channel_id=1, replica_groups=mesh['dp'=16,'tile'=32] {'tile'}, use_global_device_ids=true, to_apply=%region_5.6 | all-reduce | flops 128 | bytes 1024 | tf_op jit(solution)/shard_map/psum | solution.py:50
  126.6 144.8 %all-reduce.4.cloned.1.call-done = f32[16,8,192]{2,0,1:T(8,128)} async-done(((f32[16,8,192]{2,0,1:T(8,128)}), f32[16,8,192]{2,0,1:T(8,128)}) %all-reduce.4.cloned.1.call-update) | async-done | bytes 98320 | tf_op jit(solution)/shard_map/psum | solution.py:50
  271.3 1.1 multiply_reduce_fusion
  272.4 0.1 copy.15
  272.5 0.1 reshape.66
  272.6 0.0 copy-start.3
  272.7 0.1 fusion.33
  272.7 68.4 %all-gather.2.cloned.1.call-done = bf16[1536,512]{1,0:T(8,128)(2,1)} async-done(((bf16[48,512]{1,0:T(8,128)(2,1)}), bf16[1536,512]{1,0:T(8,128)(2,1)}) %all-gather.2.cloned.1.call-update) | async-done | bytes 1572880 | tf_op jit(solution)/shard_map/all_gather | solution.py:59
  341.2 1.8 fusion.8
  343.0 0.0 copy-done.6
  343.0 0.8 fusion.30
  343.7 2.9 multiply_reduce_fusion.1
  346.6 0.1 subtract_divide_fusion
  346.7 0.1 reshape.68
  346.8 0.0 copy-done.3
  346.8 6.0 %convert_multiply_fusion = f32[1024,1536]{1,0:T(8,128)} fusion(bf16[1024,1536]{1,0:T(8,128)(2,1)} %param.8, f32[16,1536]{1,0:T(8,128)S(1)} %subtract_divide_fusion, s32[1024]{0:T(1024)S(1)} %bitcast.39), kind=kOutput, calls=%fused_computation | convolution fusion | flops 305152000 | bytes 9539584 | tf_op jit(solution)/shard_map/dot_general | solution.py:78
  352.8 0.9 fusion.25
  353.8 0.0 all-reduce.6.cloned.1.call-update
  353.8 0.1 fusion.6
  353.9 0.3 select_reduce_fusion.2
  354.2 6.5 %copy.16 = f32[1024,1536]{0,1:T(8,128)} copy(f32[1024,1536]{1,0:T(8,128)} %convert_multiply_fusion) | data formatting | bytes 12582912 | tf_op jit(solution)/shard_map/mul | solution.py:80
  360.8 3.4 reduce_sum.90
  364.1 0.5 fusion.14
  364.6 0.1 fusion.28
  364.8 33.9 %all-reduce = (f32[512]{0:T(512)}, f32[]{:T(128)}) all-reduce(f32[512]{0:T(512)S(1)} %bitcast.40, f32[]{:T(128)} %get-tuple-element.10), channel_id=1, replica_groups=mesh['dp'=16,'tile'=32] {'dp'}, use_global_device_ids=true, to_apply=%region_14.15 | all-reduce | flops 513 | bytes 4104 | tf_op jit(solution)/shard_map/psum | solution.py:70
  399.4 105.5 %psum.45 = f32[512,8]{0,1:T(8,128)} all-reduce(f32[512,8]{0,1:T(8,128)S(1)} %fusion.14), channel_id=1, replica_groups=mesh['dp'=16,'tile'=32] {'dp','tile'}, use_global_device_ids=true, to_apply=%region_13.14 | all-reduce | flops 4096 | bytes 32768 | tf_op jit(solution)/shard_map/psum | solution.py:85
  504.9 0.0 all-reduce.6.cloned.1.call-done
  504.9 1.5 copy.23
  (6 shorter events, 0.1 us)
Async XLA Ops:
  7.2 5.5 %copy-start = (bf16[1536,512]{1,0:T(8,128)(2,1)S(1)}, bf16[1536,512]{1,0:T(8,128)(2,1)}, u32[]{:S(2)}) copy-start(bf16[1536,512]{1,0:T(8,128)(2,1)} %param.11) | copy-start | bytes 4718596
  7.2 264.2 %all-reduce.4.cloned.1.call-start = ((), (), s32[]{:S(2)}) async-start(), calls=%async_computation | async-start | bytes 262144 | tf_op jit(solution)/shard_map/psum | solution.py:50
  12.7 3.8 copy-start.2
  12.7 3.8 copy-start.7
  16.5 2.3 copy-start.4
  72.7 3.2 copy-start.1
  75.9 2.4 copy-start.5
  77.5 265.5 %copy-start.6 = (s32[1,16]{1,0:T(1,128)S(1)}, s32[1,16]{1,0:T(1,128)}, u32[]{:S(2)}) copy-start(s32[1,16]{1,0:T(1,128)} %param.10) | copy-start | bytes 196
  77.5 263.6 %all-gather.2.cloned.1.call-start = ((), (), s32[]{:S(2)}) async-start(), calls=%async_computation.1 | async-start | bytes 1622016 | tf_op jit(solution)/shard_map/all_gather | solution.py:59
  78.3 426.6 %all-reduce.6.cloned.1.call-start = ((), (), s32[]{:S(2)}) async-start(), calls=%async_computation.2 | async-start | bytes 196608 | tf_op jit(solution)/shard_map/psum | solution.py:70
  272.6 74.2 %copy-start.3 = (s32[1,1024]{1,0:T(1,128)S(1)}, s32[1,1024]{1,0:T(1,128)}, u32[]{:S(2)}) copy-start(s32[1,1024]{1,0:T(1,128)} %param.9) | copy-start | bytes 12292
Sparse Core Ops, SparseCore 0:
  77.6 193.6 all-reduce.3
  273.7 67.4 all-gather.1
  353.9 107.6 all-reduce.5
where the time goes:
time: 515 us; the launch traced here: 514 us
  blocking collectives  241 us (47%)
  waiting for transfers between devices  214 us (42%)
  matrix products  24.1 us (5%)
  between operations  15.7 us (3%)
  local copies, waits for them, and re-layouts  13 us (3%)
  other arithmetic  6.35 us (1%)
    psum x1, waiting for transfers between devices, body(): totals, pooled = lax.psum((totals, pooled), 'tile')  145 us
    psum x1, blocking collectives, body(): grad_score = lax.psum(score_part, ('dp', 'tile'))  105 us
    all_gather x1, waiting for transfers between devices, body(): whole_w1 = lax.all_gather(head_w1, 'tile', axis=0, tiled=True)  68.4 us
    pmax x1, blocking collectives, body(): global_max = lax.pmax(local_max, 'tile')  53.3 us
    psum x1, blocking collectives, body(): totals, pooled = lax.psum((totals, pooled), 'tile')  48.1 us
    psum x1, blocking collectives, body(): lax.psum((rows_part, w2_part, jnp.sum(loss_terms)), 'dp')  33.9 us
  transfers between devices with their start and end apart: 3, of which 2 were waited for; matrix products, arithmetic and copies ran while one was open for 2% of the time, Pallas kernels for 0%

commit v1 on v0

v1 whole, which is shorter than its diff:
```python
import functools

import jax
import jax.numpy as jnp
from jax import lax
from jax.experimental import pallas as pl
from jax.experimental.pallas import tpu as pltpu
from jax.sharding import PartitionSpec as P

f32, bf16 = jnp.float32, jnp.bfloat16
MESH = pl.DeviceIdType.MESH
LOW = -3.0e38
BLOCK = 256
NN = (((1,), (0,)), ((), ()))
NT = (((1,), (1,)), ((), ()))
TN = (((0,), (0,)), ((), ()))


def matmul(a, b, dims=NN):
    return lax.dot_general(a, b, dims, preferred_element_type=f32)


def split(values):
    upper = values.astype(bf16)
    return upper, (values - upper.astype(f32)).astype(bf16)


def gelu_slope(values, phi):
    return phi + values * jnp.exp(-0.5 * values * values) * 0.3989422804014327


def remote(src, dst, send, recv, **where):
    return pltpu.make_async_remote_copy(
        src_ref=src, dst_ref=dst, send_sem=send, recv_sem=recv,
        device_id=where, device_id_type=MESH,
    )


def drain(ref, sem):
    pltpu.make_async_copy(ref, ref, sem).wait()


def kernel(
    tiles_hbm, seg_ref, lab_ref, v_hbm, u_hbm, sw_ref, w1_hbm, w2_ref,
    gw1_ref, gs_ref, gw2_ref, loss_ref,
    tiles, wv, wu, gated, scores, expo, w1, delta,
    swap_out, swap_in, red_out, red_in, own_half, other_half,
    wide, msg, gs_out, gs_in, gd, ga,
    load_sem, w1_sem, half_sem, red_sem, all_sem, msg_sem, gs_sem, gd_sem, ga_sem,
):
    d, t = lax.axis_index("dp"), lax.axis_index("tile")
    z, c = t // 2, t % 2
    other_t = 2 * z + 1 - c
    dx, dy = d // 4, d % 4
    rows = tiles.shape[0]

    barrier = pltpu.get_barrier_semaphore()

    def greet_tile(i, carry):
        pl.semaphore_signal(barrier, inc=1, device_id={"tile": (t + 1 + i) % 32}, device_id_type=MESH)
        return carry

    def greet_dp(i, carry):
        pl.semaphore_signal(barrier, inc=1, device_id={"dp": (d + 1 + i) % 16}, device_id_type=MESH)
        return carry

    lax.fori_loop(0, 31, greet_tile, 0)
    lax.fori_loop(0, 15, greet_dp, 0)

    loads = [
        pltpu.make_async_copy(v_hbm, wv, load_sem.at[0]),
        pltpu.make_async_copy(u_hbm, wu, load_sem.at[1]),
    ]
    for b in range(rows // BLOCK):
        part = pl.ds(b * BLOCK, BLOCK)
        loads.append(pltpu.make_async_copy(tiles_hbm.at[part], tiles.at[part], load_sem.at[2 + b]))
    own_w1 = pltpu.make_async_copy(
        w1_hbm.at[:, pl.ds(pl.multiple_of(dx * 128, 128), 128)],
        w1.at[dx, z // 4, z % 4, c], load_sem.at[7],
    )
    for load in loads:
        load.start()

    pl.semaphore_wait(barrier, 46)

    def w1_first(i):
        peer = (z + 1 + i) % 16
        return remote(
            w1_hbm.at[:, pl.ds(pl.multiple_of(dx * 128, 128), 128)],
            w1.at[dx, z // 4, z % 4, c], w1_sem.at[0], w1_sem.at[1], tile=2 * peer + c,
        )

    @pl.when(z % 4 == dy)
    def _():
        own_w1.start()

        def go(i, carry):
            w1_first(i).start()
            return carry

        lax.fori_loop(0, 15, go, 0)

    loads[0].wait()
    loads[1].wait()

    def scorer(b):
        part = pl.ds(b * BLOCK, BLOCK)
        x = tiles[part, :]
        tanh_part = jnp.tanh(matmul(x, wv[...]))
        gate_part = 0.5 + 0.5 * jnp.tanh(0.5 * matmul(x, wu[...]))
        low = (tanh_part * gate_part).astype(bf16)
        gated[part, :] = low
        scores[:, part] = matmul(sw_ref[...], low, NT)

    loads[2].wait()
    scorer(0)

    @pl.when(z % 4 == dy)
    def _():
        own_w1.wait()
        for _ in range(1):
            drain(w1.at[0, pl.ds(0, 3), 0, 0], w1_sem.at[1])

    @pl.when(z % 4 != dy)
    def _():
        drain(w1.at[0, :, 0, 0], w1_sem.at[1])

    def w1_second(i):
        part = w1.at[dx, :, dy, c]
        return remote(part, part, w1_sem.at[2], w1_sem.at[3], dp=(d + 1 + i) % 16)

    def go_second(i, carry):
        w1_second(i).start()
        return carry

    lax.fori_loop(0, 15, go_second, 0)

    for b in range(1, rows // BLOCK):
        loads[2 + b].wait()
        scorer(b)

    member = lax.broadcasted_iota(jnp.int32, (16, rows), 0) == seg_ref[...]
    lane = lax.broadcasted_iota(jnp.int32, (16, 128), 1)
    top = jnp.full((16, 128), LOW, f32)
    total = jnp.zeros((16, 128), f32)
    for k in range(8):
        score = jnp.broadcast_to(scores[k : k + 1, :], (16, rows))
        peak = jnp.max(jnp.where(member, score, LOW), axis=1, keepdims=True)
        term = jnp.where(member, jnp.exp(score - peak), 0.0)
        expo[16 * k : 16 * k + 16, :] = term
        top = jnp.where(lane == k, peak, top)
        total = jnp.where(lane == k, jnp.sum(term, axis=1, keepdims=True), total)

    blocks = []
    for q in range(4):
        upper, lower = split(expo[32 * q : 32 * q + 32, :])
        both = matmul(jnp.concatenate([upper, lower], axis=0), tiles[:, 384 * q : 384 * q + 384])
        both = both[:32] + both[32:]
        first, second = both[:16], both[16:]
        blocks += [
            first[:, :128],
            jnp.where(lane < 64, first[:, 128:256], second[:, 128:256]),
            second[:, 256:],
        ]

    def pick(a, b):
        return jnp.where(c == 0, a, b)

    def strided(j):
        return pl.ds(j, 16, stride=8)

    for j in range(6):
        swap_out[strided(j), :] = pick(blocks[6 + j], blocks[j])
    swap_out[strided(6), :] = total
    swap_out[strided(7), :] = top
    swap = remote(swap_out, swap_in, half_sem.at[0], half_sem.at[1], tile=other_t)
    swap.start()
    mine = [pick(blocks[j], blocks[6 + j]) for j in range(6)]
    swap.wait()

    low_lane = lane < 64

    def spread(table):
        heads = [pick(table[:, k : k + 1], table[:, 4 + k : 5 + k]) for k in range(4)]
        n = table.shape[0]
        heads = [jnp.broadcast_to(h, (n, 128)) for h in heads]
        low = low_lane[:n]
        return [
            heads[0], jnp.where(low, heads[0], heads[1]), heads[1],
            heads[2], jnp.where(low, heads[2], heads[3]), heads[3],
        ]

    top_other = swap_in[strided(7), :]
    pair_top = jnp.maximum(top, top_other)
    scale, scale_other = jnp.exp(top - pair_top), jnp.exp(top_other - pair_top)
    wide_own, wide_other = spread(scale), spread(scale_other)
    for j in range(6):
        red_out[strided(j), :] = mine[j] * wide_own[j] + swap_in[strided(j), :] * wide_other[j]
    red_out[strided(6), :] = total * scale + swap_in[strided(6), :] * scale_other
    red_out[strided(7), :] = pair_top

    def eight(i):
        return pl.ds(pl.multiple_of(8 * i, 8), 8)

    def reduce_copy(i):
        peer = (z + 1 + i) % 16
        return remote(red_out.at[eight(peer)], red_in.at[eight(z)], red_sem.at[0], red_sem.at[1], tile=2 * peer + c)

    def go_reduce(i, carry):
        reduce_copy(i).start()
        return carry

    lax.fori_loop(0, 15, go_reduce, 0)
    red_in[eight(z), :] = red_out[eight(z), :]

    drain(tiles_hbm.at[pl.ds(0, 240)], w1_sem.at[3])
    w1_third = remote(w1.at[:, :, :, c], w1.at[:, :, :, c], w1_sem.at[4], w1_sem.at[5], tile=other_t)
    w1_third.start()

    drain(red_in.at[pl.ds(0, 120)], red_sem.at[1])
    tops = red_in[strided(7), :]
    slide_top = jnp.max(tops, axis=0, keepdims=True)
    scale = jnp.exp(tops - slide_top)
    slide_total = jnp.sum(red_in[strided(6), :] * scale, axis=0, keepdims=True)
    wide_scale, wide_total = spread(scale), spread(slide_total)
    tile_rows = [
        jnp.sum(red_in[strided(j), :] * wide_scale[j], axis=0, keepdims=True) / wide_total[j]
        for j in range(6)
    ]
    own_half[eight(z), :] = jnp.concatenate(tile_rows + [slide_total, slide_top], axis=0)

    def gather_copy(i):
        peer = (z + 1 + i) % 16
        return remote(own_half.at[eight(z)], own_half.at[eight(z)], all_sem.at[0], all_sem.at[1], tile=2 * peer + c)

    def go_gather(i, carry):
        gather_copy(i).start()
        return carry

    lax.fori_loop(0, 15, go_gather, 0)
    drain(own_half.at[pl.ds(0, 120)], all_sem.at[1])
    relay = remote(own_half, other_half, half_sem.at[2], half_sem.at[3], tile=other_t)
    relay.start()
    w1_third.wait()
    relay.wait()

    left, right = [], []
    for j in range(6):
        a, b = own_half[strided(j), :], other_half[strided(j), :]
        left.append(pick(a, b))
        right.append(pick(b, a))
    pooled = jnp.concatenate(left + right, axis=1)
    slide_total, slide_top = own_half[strided(6), :], own_half[strided(7), :]
    width = pooled.shape[1]
    root_mean = jnp.sqrt(jnp.sum(pooled * pooled, axis=1, keepdims=True) / width + 1e-5)
    normed = pooled / root_mean
    normed_low = normed.astype(bf16)
    whole = jnp.concatenate([w1[x].reshape(width, 128) for x in range(4)], axis=1)
    pre_act = matmul(normed_low, whole)
    phi = 0.5 * (1.0 + lax.erf(pre_act * 0.7071067811865476))
    hidden = pre_act * phi
    w2_float = w2_ref[...].astype(f32)
    logits = jnp.sum(hidden * w2_float, axis=1, keepdims=True)
    square = lax.broadcasted_iota(jnp.int32, (16, 16), 0) == lax.broadcasted_iota(jnp.int32, (16, 16), 1)
    target = jnp.sum(
        jnp.where(square, jnp.broadcast_to(lab_ref[...], (16, 16)).astype(f32), 0.0), axis=1, keepdims=True
    )
    soft = jnp.exp(-jnp.abs(logits))
    loss_part = jnp.sum(jnp.maximum(logits, 0.0) + jnp.log1p(soft) - target * logits, axis=0, keepdims=True)
    logit_grad = jnp.where(logits >= 0.0, 1.0, soft) / (1.0 + soft) - target
    w2_part = jnp.sum(logit_grad * hidden, axis=0, keepdims=True)
    pre_grad = logit_grad * w2_float * gelu_slope(pre_act, phi)

    wide[:, :width] = normed_low.astype(f32)
    wide[:, width:] = jnp.zeros((16, 128), f32)
    first = 48 * t
    window = wide[:, pl.ds(pl.multiple_of(first // 128 * 128, 128), 256)].astype(bf16)
    chosen = lax.broadcasted_iota(jnp.int32, (256, 128), 0) == (
        lax.broadcasted_iota(jnp.int32, (256, 128), 1) + first % 128
    )
    normed_own = matmul(window, jnp.where(chosen, 1.0, 0.0).astype(bf16))
    sub = lax.broadcasted_iota(jnp.int32, (16, 128), 0)
    extra = jnp.zeros((16, 128), f32)
    for j in range(5):
        piece = w2_part[:, 128 * j : 128 * j + 128] if j < 4 else jnp.broadcast_to(loss_part, (1, 128))
        upper = piece.astype(bf16).astype(f32)
        extra = jnp.where(sub == j, upper, extra)
        extra = jnp.where(sub == 8 + j, piece - upper, extra)
    msg[d] = jnp.concatenate([pre_grad, normed_own, extra], axis=1).astype(bf16)

    def message(i):
        return remote(msg.at[d], msg.at[d], msg_sem.at[0], msg_sem.at[1], dp=(d + 1 + i) % 16)

    def go_message(i, carry):
        message(i).start()
        return carry

    lax.fori_loop(0, 15, go_message, 0)

    upper, lower = split(pre_grad)
    both = matmul(jnp.concatenate([upper, lower], axis=0), whole, NT)
    norm_grad = both[:16] + both[16:]
    pool_grad = (norm_grad - normed * (jnp.sum(norm_grad * normed, axis=1, keepdims=True) / width)) / root_mean

    product = pooled * pool_grad
    weight = jnp.exp(top - slide_top) / slide_total
    lane_pair = lax.broadcasted_iota(jnp.int32, (16, 384), 1)
    for q in range(4):
        grads = pool_grad[:, 384 * q : 384 * q + 384]
        terms = product[:, 384 * q : 384 * q + 384]
        pair = jnp.concatenate(
            [jnp.where(lane_pair < 192, grads, 0.0), jnp.where(lane_pair >= 192, grads, 0.0)], axis=0
        )
        upper, lower = split(pair)
        both = matmul(jnp.concatenate([upper, lower], axis=0), tiles[:, 384 * q : 384 * q + 384], NT)
        both = both[:32] + both[32:]
        for half in range(2):
            k = 2 * q + half
            side = lane_pair < 192 if half == 0 else lane_pair >= 192
            inner = jnp.sum(jnp.where(side, terms, 0.0), axis=1, keepdims=True)
            change = expo[16 * k : 16 * k + 16, :] * ((both[16 * half : 16 * half + 16] - inner) * weight[:, k : k + 1])
            delta[k : k + 1, :] = jnp.sum(change, axis=0, keepdims=True)

    upper, lower = split(delta[...])
    both = matmul(jnp.concatenate([upper, lower], axis=0), gated[...])
    score_part = both[:8] + both[8:]

    for k in range(8):
        for j in range(4):
            gs_out[4 * k + j] = score_part[k : k + 1, 128 * j : 128 * j + 128]

    def gs_reduce(i):
        peer = (t + 1 + i) % 32
        return remote(gs_out.at[peer], gs_in.at[t], gs_sem.at[0], gs_sem.at[1], tile=peer)

    def go_gs_reduce(i, carry):
        gs_reduce(i).start()
        return carry

    lax.fori_loop(0, 31, go_gs_reduce, 0)
    gs_in[t] = gs_out[t]

    drain(msg.at[pl.ds(0, 15)], msg_sem.at[1])
    grads = msg[:, :, 0:512].reshape(256, 512)
    own = msg[:, :, 512:640].reshape(256, 128)
    gw1_ref[...] = matmul(own, grads, TN)[:48]
    sums = jnp.sum(msg[:, :, 640:768].astype(f32), axis=0)
    sums = sums[:8] + sums[8:]
    gw2_ref[...] = jnp.concatenate([sums[j : j + 1] for j in range(4)], axis=1)
    loss_ref[...] = sums[4:5, 0:1] * (1.0 / 256.0)

    drain(gs_in.at[pl.ds(0, 31)], gs_sem.at[1])
    gd[d] = jnp.sum(gs_in[...], axis=0)

    def gs_dp(i):
        return remote(gd.at[d], gd.at[d], gd_sem.at[0], gd_sem.at[1], dp=(d + 1 + i) % 16)

    def go_gs_dp(i, carry):
        gs_dp(i).start()
        return carry

    lax.fori_loop(0, 15, go_gs_dp, 0)
    drain(gd.at[pl.ds(0, 15)], gd_sem.at[1])
    ga[t] = jnp.sum(gd[...], axis=0)

    def gs_gather(i):
        peer = (t + 1 + i) % 32
        return remote(ga.at[t], ga.at[t], ga_sem.at[0], ga_sem.at[1], tile=peer)

    def go_gs_gather(i, carry):
        gs_gather(i).start()
        return carry

    lax.fori_loop(0, 31, go_gs_gather, 0)
    drain(ga.at[pl.ds(0, 31)], ga_sem.at[1])
    gs_ref[...] = ga[...]

    @pl.when(z % 4 == dy)
    def _():
        def done(i, carry):
            w1_first(i).wait_send()
            return carry

        lax.fori_loop(0, 15, done, 0)

    drain(tiles_hbm.at[pl.ds(0, 240)], w1_sem.at[2])
    drain(red_in.at[pl.ds(0, 120)], red_sem.at[0])
    drain(own_half.at[pl.ds(0, 120)], all_sem.at[0])
    drain(msg.at[pl.ds(0, 15)], msg_sem.at[0])
    drain(gs_in.at[pl.ds(0, 31)], gs_sem.at[0])
    drain(gd.at[pl.ds(0, 15)], gd_sem.at[0])
    drain(ga.at[pl.ds(0, 31)], ga_sem.at[0])


def body(tiles, slide_of_tile, labels, attn_v, attn_u, score_w, head_w1, head_w2):
    rows, width = tiles.shape
    hid = attn_v.shape[1]
    vmem, hbm = pl.BlockSpec(memory_space=pltpu.VMEM), pl.BlockSpec(memory_space=pl.ANY)
    dma = pltpu.SemaphoreType.DMA
    grad_w1, grad_score, grad_w2, loss = pl.pallas_call(
        kernel,
        out_shape=(
            jax.ShapeDtypeStruct((48, hid), f32),
            jax.ShapeDtypeStruct((32, 1, 128), f32),
            jax.ShapeDtypeStruct((1, hid), f32),
            jax.ShapeDtypeStruct((1, 1), f32),
        ),
        in_specs=[hbm, vmem, vmem, hbm, hbm, vmem, hbm, vmem],
        out_specs=(vmem, vmem, vmem, vmem),
        scratch_shapes=[
            pltpu.VMEM((rows, width), bf16),
            pltpu.VMEM((width, hid), bf16),
            pltpu.VMEM((width, hid), bf16),
            pltpu.VMEM((rows, hid), bf16),
            pltpu.VMEM((8, rows), f32),
            pltpu.VMEM((128, rows), f32),
            pltpu.VMEM((4, 4, 4, 2, 48, 128), bf16),
            pltpu.VMEM((8, rows), f32),
            pltpu.VMEM((128, 128), f32),
            pltpu.VMEM((128, 128), f32),
            pltpu.VMEM((128, 128), f32),
            pltpu.VMEM((128, 128), f32),
            pltpu.VMEM((128, 128), f32),
            pltpu.VMEM((128, 128), f32),
            pltpu.VMEM((16, width + 128), f32),
            pltpu.VMEM((16, 16, 768), bf16),
            pltpu.VMEM((32, 1, 128), f32),
            pltpu.VMEM((32, 1, 128), f32),
            pltpu.VMEM((16, 1, 128), f32),
            pltpu.VMEM((32, 1, 128), f32),
            dma((8,)), dma((6,)), dma((4,)), dma((2,)), dma((2,)), dma((2,)), dma((2,)), dma((2,)), dma((2,)),
        ],
        compiler_params=pltpu.CompilerParams(
            collective_id=0, has_side_effects=True, vmem_limit_bytes=48 * 1024 * 1024
        ),
    )(tiles, slide_of_tile, labels, attn_v, attn_u, score_w.T, head_w1, head_w2.reshape(1, hid))
    return grad_w1, grad_score.reshape(8, hid).T, grad_w2.reshape(hid), loss.reshape(())


def solution(mesh):
    return jax.shard_map(
        body,
        mesh=mesh,
        in_specs=(
            P(("dp", "tile"), None),
            P("dp", "tile"),
            P("dp", None),
            P(),
            P(),
            P(),
            P("tile", None),
            P(),
        ),
        out_specs=(P("tile", None), P(), P(), P()),
        check_vma=False,
    )
```

time: 515 us -> 84.2 us (0.16)
  blocking collectives: 241 us -> 0 us
  waiting for transfers between devices: 214 us -> 0 us
  Pallas kernels: 0 us -> 72.1 us
  matrix products: 24.1 us -> 0 us
  between operations: 15.7 us -> 2.4 us
  other arithmetic: 6.35 us -> 0.68 us
    psum x3 -> x0, blocking collectives: 187 us -> none  [the longest x1 105 us: body(): grad_score = lax.psum(score_part, ('dp', 'tile'))]
    psum x2 -> x0, waiting for transfers between devices: 145 us -> none  [the longest x1 145 us: body(): totals, pooled = lax.psum((totals, pooled), 'tile')]
    pallas_call x0 -> x1, Pallas kernels: none -> 72.1 us  [body(): pl.pallas_call(kernel, out_shape=(jax.ShapeDtypeStruct((48, hid), f32), j...]
    all_gather x1 -> x0, waiting for transfers between devices: 68.4 us -> none  [body(): whole_w1 = lax.all_gather(head_w1, 'tile', axis=0, tiled=True)]
    pmax x1 -> x0, blocking collectives: 53.3 us -> none  [body(): global_max = lax.pmax(local_max, 'tile')]
    dot_general x12 -> x0, matrix products: 24.1 us -> none  [the longest x1 6.02 us: body(): tile_grad = jnp.dot(onehot, flat_grad, precision=highest)]
    mul x1 -> x0, local copies, waits for them, and re-layouts: 6.53 us -> none  [body(): tiles.astype(jnp.float32) * tile_grad]
    reduce_sum x6 -> x0, other arithmetic: 5.17 us -> none  [the longest x1 3.37 us: body(): jnp.sum((tiles.astype(jnp.float32) * tile_grad).reshape(row_count, head_c...]
  transfers between devices with their start and end apart: 3 -> 0, of which waited for: 2 -> 0; matrix products, arithmetic and copies ran while one was open for 2% -> 0% of each run, Pallas kernels for 0% -> 0%
where the time goes in v1:
time: 84.2 us; the launch traced here: 83.9 us
  Pallas kernels  72.1 us (86%)
  local copies, waits for them, and re-layouts  8.67 us (10%)
  between operations  2.4 us (3%)
    pallas_call x1, Pallas kernels, body(): pl.pallas_call(kernel, out_shape=(jax.ShapeDtypeStruct((48, hid), f32), j...  72.1 us
    unnamed x14, local copies, waits for them, and re-layouts  6.87 us

profile of v1, /device:TPU:1, one launch (start us, length us, event | category | flops | bytes accessed | tf_op | source)
XLA Modules:
  0.0 83.9 jit_solution(3497793980198604716)
XLA Ops:
  0.6 0.7 reshape.20.w2_ref
  1.3 0.0 copy-start
  1.3 1.4 %copy-done = bf16[1536,512]{1,0:T(8,128)(2,1)S(1)} copy-done((bf16[1536,512]{1,0:T(8,128)(2,1)S(1)}, bf16[1536,512]{1,0:T(8,128)(2,1)}, u32[]{:S(2)}) %copy-start) | copy-done | bytes 1572888
  2.7 0.0 copy-start.1
  2.7 1.4 %copy-done.1 = bf16[1536,512]{1,0:T(8,128)(2,1)S(1)} copy-done((bf16[1536,512]{1,0:T(8,128)(2,1)S(1)}, bf16[1536,512]{1,0:T(8,128)(2,1)}, u32[]{:S(2)}) %copy-start.1) | copy-done | bytes 1572888
  4.1 0.0 copy-start.2
  4.1 0.8 copy-done.2
  4.9 0.0 copy-start.3
  4.9 0.7 copy-done.3
  5.6 0.0 copy-start.4
  5.6 0.7 copy-done.4
  6.3 0.0 copy-start.5
  6.3 0.7 copy-done.5
  7.0 72.1 %shard_map.111 = (f32[48,512]{1,0:T(8,128)S(1)}, f32[32,1,128]{2,1,0:T(1,128)S(1)}, f32[1,512]{1,0:T(1,128)S(1)}, f32[1,1]{1,0:T(1,128)}) custom-call(bf16[1024,1536]{1,0:T(8,128)(2,1)} %tiles_hbm.1, s32[1,1024]{1,0:T(1,128)S(1)} %copy-done.4, s32[1,16]{1,0:T(1,128)S(1)} %copy-done.5, bf16[1536,512]{1,0:T(8,128)(2,1)S(1)} %copy-done, ...), custom_call_target="tpu_custom_call" | custom-call | tf_op jit(solution)/shard_map/pallas_call | solution.py:400
  79.1 0.5 broadcast.3
  79.6 0.7 reduce.3
  80.3 0.6 reshape.21
  80.9 0.6 copy.15
  81.6 0.6 copy.16
Async XLA Ops:
  1.3 1.4 %copy-start = (bf16[1536,512]{1,0:T(8,128)(2,1)S(1)}, bf16[1536,512]{1,0:T(8,128)(2,1)}, u32[]{:S(2)}) copy-start(bf16[1536,512]{1,0:T(8,128)(2,1)} %v_hbm.1) | copy-start | bytes 4718596
  2.7 1.4 %copy-start.1 = (bf16[1536,512]{1,0:T(8,128)(2,1)S(1)}, bf16[1536,512]{1,0:T(8,128)(2,1)}, u32[]{:S(2)}) copy-start(bf16[1536,512]{1,0:T(8,128)(2,1)} %u_hbm.1) | copy-start | bytes 4718596
  4.1 0.8 copy-start.2
  4.9 0.7 copy-start.3
  5.6 0.7 copy-start.4
  6.3 0.7 copy-start.5

commit v2 on v1

--- a/solution.py
+++ b/solution.py
@@ -41,31 +41,48 @@
 
 
 def kernel(
-    tiles_hbm, seg_ref, lab_ref, v_hbm, u_hbm, sw_ref, w1_hbm, w2_ref,
+    tiles_hbm, seg_hbm, lab_hbm, v_hbm, u_hbm, sw_hbm, w1_hbm, w2_hbm,
     gw1_ref, gs_ref, gw2_ref, loss_ref,
-    tiles, wv, wu, gated, scores, expo, w1, delta,
+    tiles, seg, lab, wv, wu, sw, w2,
+    gated, scores, expo, w1, delta,
     swap_out, swap_in, red_out, red_in, own_half, other_half,
-    wide, msg, gs_out, gs_in, gd, ga,
-    load_sem, w1_sem, half_sem, red_sem, all_sem, msg_sem, gs_sem, gd_sem, ga_sem,
+    wide, msg, gs_out, gs_in, gz, ga,
+    load_sem, w1_sem, half_sem, red_sem, all_sem, msg_sem, gs_sem, gz_sem, ga_sem,
 ):
     d, t = lax.axis_index("dp"), lax.axis_index("tile")
     z, c = t // 2, t % 2
     other_t = 2 * z + 1 - c
     dx, dy = d // 4, d % 4
     rows = tiles.shape[0]
+    sent = []
+
+    def finish():
+        for wait in sent:
+            wait()
+
+    def loop(count, step):
+        def go(i, carry):
+            step(i)
+            return carry
+
+        lax.fori_loop(0, count, go, 0)
 
     barrier = pltpu.get_barrier_semaphore()
 
-    def greet_tile(i, carry):
-        pl.semaphore_signal(barrier, inc=1, device_id={"tile": (t + 1 + i) % 32}, device_id_type=MESH)
-        return carry
-
-    def greet_dp(i, carry):
-        pl.semaphore_signal(barrier, inc=1, device_id={"dp": (d + 1 + i) % 16}, device_id_type=MESH)
-        return carry
-
-    lax.fori_loop(0, 31, greet_tile, 0)
-    lax.fori_loop(0, 15, greet_dp, 0)
+    place = 2 * d + c
+
+    def plane_peer(i):
+        p = (place + 1 + i) % 32
+        return p, {"dp": p // 2, "tile": 2 * z + p % 2}
+
+    def z_peer(i):
+        return {"tile": 2 * ((z + 1 + i) % 16) + c}
+
+    def greet(who):
+        pl.semaphore_signal(barrier, inc=1, device_id=who, device_id_type=MESH)
+
+    loop(31, lambda i: greet(plane_peer(i)[1]))
+    loop(15, lambda i: greet(z_peer(i)))
 
     loads = [
         pltpu.make_async_copy(v_hbm, wv, load_sem.at[0]),
@@ -74,14 +91,19 @@
     for b in range(rows // BLOCK):
         part = pl.ds(b * BLOCK, BLOCK)
         loads.append(pltpu.make_async_copy(tiles_hbm.at[part], tiles.at[part], load_sem.at[2 + b]))
+    small = [
+        pltpu.make_async_copy(sw_hbm, sw, load_sem.at[8]),
+        pltpu.make_async_copy(seg_hbm, seg, load_sem.at[9]),
+        pltpu.make_async_copy(lab_hbm, lab, load_sem.at[10]),
+        pltpu.make_async_copy(w2_hbm, w2, load_sem.at[11]),
+    ]
     own_w1 = pltpu.make_async_copy(
         w1_hbm.at[:, pl.ds(pl.multiple_of(dx * 128, 128), 128)],
         w1.at[dx, z // 4, z % 4, c], load_sem.at[7],
     )
-    for load in loads:
+    for load in loads + small:
         load.start()
 
-    pl.semaphore_wait(barrier, 46)
 
     def w1_first(i):
         peer = (z + 1 + i) % 16
@@ -90,18 +112,48 @@
             w1.at[dx, z // 4, z % 4, c], w1_sem.at[0], w1_sem.at[1], tile=2 * peer + c,
         )
 
-    @pl.when(z % 4 == dy)
-    def _():
-        own_w1.start()
-
-        def go(i, carry):
-            w1_first(i).start()
-            return carry
-
-        lax.fori_loop(0, 15, go, 0)
+    def w1_second(i):
+        part = w1.at[dx, :, dy, c]
+        return remote(part, part, w1_sem.at[2], w1_sem.at[3], dp=(d + 1 + i) % 16)
+
+    w1_third = remote(w1.at[:, :, :, c], w1.at[:, :, :, c], w1_sem.at[4], w1_sem.at[5], tile=other_t)
+
+    def w1_start():
+        @pl.when(z % 4 == dy)
+        def _():
+            own_w1.start()
+            loop(15, lambda i: w1_first(i).start())
+
+        def wait_first():
+            @pl.when(z % 4 == dy)
+            def _():
+                loop(15, lambda i: w1_first(i).wait_send())
+
+        sent.append(wait_first)
+
+    def w1_middle():
+        @pl.when(z % 4 == dy)
+        def _():
+            own_w1.wait()
+            drain(w1.at[0, pl.ds(0, 3), 0, 0], w1_sem.at[1])
+
+        @pl.when(z % 4 != dy)
+        def _():
+            drain(w1.at[0, :, 0, 0], w1_sem.at[1])
+
+        loop(15, lambda i: w1_second(i).start())
+        sent.append(lambda: drain(tiles_hbm.at[pl.ds(0, 240)], w1_sem.at[2]))
+
+    def w1_last():
+        drain(tiles_hbm.at[pl.ds(0, 240)], w1_sem.at[3])
+        w1_third.start()
+
+    def w1_end():
+        w1_third.wait()
 
     loads[0].wait()
     loads[1].wait()
+    small[0].wait()
 
     def scorer(b):
         part = pl.ds(b * BLOCK, BLOCK)
@@ -110,36 +162,17 @@
         gate_part = 0.5 + 0.5 * jnp.tanh(0.5 * matmul(x, wu[...]))
         low = (tanh_part * gate_part).astype(bf16)
         gated[part, :] = low
-        scores[:, part] = matmul(sw_ref[...], low, NT)
-
-    loads[2].wait()
-    scorer(0)
-
-    @pl.when(z % 4 == dy)
-    def _():
-        own_w1.wait()
-        for _ in range(1):
-            drain(w1.at[0, pl.ds(0, 3), 0, 0], w1_sem.at[1])
-
-    @pl.when(z % 4 != dy)
-    def _():
-        drain(w1.at[0, :, 0, 0], w1_sem.at[1])
-
-    def w1_second(i):
-        part = w1.at[dx, :, dy, c]
-        return remote(part, part, w1_sem.at[2], w1_sem.at[3], dp=(d + 1 + i) % 16)
-
-    def go_second(i, carry):
-        w1_second(i).start()
-        return carry
-
-    lax.fori_loop(0, 15, go_second, 0)
-
-    for b in range(1, rows // BLOCK):
+        scores[:, part] = matmul(sw[...], low, NT)
+
+    for b in range(rows // BLOCK):
         loads[2 + b].wait()
         scorer(b)
-
-    member = lax.broadcasted_iota(jnp.int32, (16, rows), 0) == seg_ref[...]
+    pl.semaphore_wait(barrier, 46)
+    w1_start()
+    for load in small[1:]:
+        load.wait()
+
+    member = lax.broadcasted_iota(jnp.int32, (16, rows), 0) == seg[...]
     lane = lax.broadcasted_iota(jnp.int32, (16, 128), 1)
     top = jnp.full((16, 128), LOW, f32)
     total = jnp.zeros((16, 128), f32)
@@ -206,16 +239,11 @@
         peer = (z + 1 + i) % 16
         return remote(red_out.at[eight(peer)], red_in.at[eight(z)], red_sem.at[0], red_sem.at[1], tile=2 * peer + c)
 
-    def go_reduce(i, carry):
-        reduce_copy(i).start()
-        return carry
-
-    lax.fori_loop(0, 15, go_reduce, 0)
+    loop(15, lambda i: reduce_copy(i).start())
+    sent.append(lambda: drain(red_in.at[pl.ds(0, 120)], red_sem.at[0]))
     red_in[eight(z), :] = red_out[eight(z), :]
 
-    drain(tiles_hbm.at[pl.ds(0, 240)], w1_sem.at[3])
-    w1_third = remote(w1.at[:, :, :, c], w1.at[:, :, :, c], w1_sem.at[4], w1_sem.at[5], tile=other_t)
-    w1_third.start()
+    w1_middle()
 
     drain(red_in.at[pl.ds(0, 120)], red_sem.at[1])
     tops = red_in[strided(7), :]
@@ -233,15 +261,13 @@
         peer = (z + 1 + i) % 16
         return remote(own_half.at[eight(z)], own_half.at[eight(z)], all_sem.at[0], all_sem.at[1], tile=2 * peer + c)
 
-    def go_gather(i, carry):
-        gather_copy(i).start()
-        return carry
-
-    lax.fori_loop(0, 15, go_gather, 0)
+    loop(15, lambda i: gather_copy(i).start())
+    sent.append(lambda: drain(own_half.at[pl.ds(0, 120)], all_sem.at[0]))
+    w1_last()
     drain(own_half.at[pl.ds(0, 120)], all_sem.at[1])
     relay = remote(own_half, other_half, half_sem.at[2], half_sem.at[3], tile=other_t)
     relay.start()
-    w1_third.wait()
+    w1_end()
     relay.wait()
 
     left, right = [], []
@@ -259,11 +285,11 @@
     pre_act = matmul(normed_low, whole)
     phi = 0.5 * (1.0 + lax.erf(pre_act * 0.7071067811865476))
     hidden = pre_act * phi
-    w2_float = w2_ref[...].astype(f32)
+    w2_float = w2[...].astype(f32).reshape(1, pre_act.shape[1])
     logits = jnp.sum(hidden * w2_float, axis=1, keepdims=True)
     square = lax.broadcasted_iota(jnp.int32, (16, 16), 0) == lax.broadcasted_iota(jnp.int32, (16, 16), 1)
     target = jnp.sum(
-        jnp.where(square, jnp.broadcast_to(lab_ref[...], (16, 16)).astype(f32), 0.0), axis=1, keepdims=True
+        jnp.where(square, jnp.broadcast_to(lab[...], (16, 16)).astype(f32), 0.0), axis=1, keepdims=True
     )
     soft = jnp.exp(-jnp.abs(logits))
     loss_part = jnp.sum(jnp.maximum(logits, 0.0) + jnp.log1p(soft) - target * logits, axis=0, keepdims=True)
@@ -291,11 +317,8 @@
     def message(i):
         return remote(msg.at[d], msg.at[d], msg_sem.at[0], msg_sem.at[1], dp=(d + 1 + i) % 16)
 
-    def go_message(i, carry):
-        message(i).start()
-        return carry
-
-    lax.fori_loop(0, 15, go_message, 0)
+    loop(15, lambda i: message(i).start())
+    sent.append(lambda: drain(msg.at[pl.ds(0, 15)], msg_sem.at[0]))
 
     upper, lower = split(pre_grad)
     both = matmul(jnp.concatenate([upper, lower], axis=0), whole, NT)
@@ -329,16 +352,21 @@
         for j in range(4):
             gs_out[4 * k + j] = score_part[k : k + 1, 128 * j : 128 * j + 128]
 
-    def gs_reduce(i):
-        peer = (t + 1 + i) % 32
-        return remote(gs_out.at[peer], gs_in.at[t], gs_sem.at[0], gs_sem.at[1], tile=peer)
-
-    def go_gs_reduce(i, carry):
-        gs_reduce(i).start()
-        return carry
-
-    lax.fori_loop(0, 31, go_gs_reduce, 0)
-    gs_in[t] = gs_out[t]
+    def gs_plane(i):
+        p, who = plane_peer(i)
+        return remote(gs_out.at[p], gs_in.at[place], gs_sem.at[0], gs_sem.at[1], **who)
+
+    loop(31, lambda i: gs_plane(i).start())
+    sent.append(lambda: drain(gs_in.at[pl.ds(0, 31)], gs_sem.at[0]))
+    gs_in[place] = gs_out[place]
+    drain(gs_in.at[pl.ds(0, 31)], gs_sem.at[1])
+    gz[z] = jnp.sum(gs_in[...], axis=0)
+
+    def gs_z(i):
+        return remote(gz.at[z], gz.at[z], gz_sem.at[0], gz_sem.at[1], **z_peer(i))
+
+    loop(15, lambda i: gs_z(i).start())
+    sent.append(lambda: drain(gz.at[pl.ds(0, 15)], gz_sem.at[0]))
 
     drain(msg.at[pl.ds(0, 15)], msg_sem.at[1])
     grads = msg[:, :, 0:512].reshape(256, 512)
@@ -349,68 +377,45 @@
     gw2_ref[...] = jnp.concatenate([sums[j : j + 1] for j in range(4)], axis=1)
     loss_ref[...] = sums[4:5, 0:1] * (1.0 / 256.0)
 
-    drain(gs_in.at[pl.ds(0, 31)], gs_sem.at[1])
-    gd[d] = jnp.sum(gs_in[...], axis=0)
-
-    def gs_dp(i):
-        return remote(gd.at[d], gd.at[d], gd_sem.at[0], gd_sem.at[1], dp=(d + 1 + i) % 16)
-
-    def go_gs_dp(i, carry):
-        gs_dp(i).start()
-        return carry
-
-    lax.fori_loop(0, 15, go_gs_dp, 0)
-    drain(gd.at[pl.ds(0, 15)], gd_sem.at[1])
-    ga[t] = jnp.sum(gd[...], axis=0)
+    drain(gz.at[pl.ds(0, 15)], gz_sem.at[1])
+    ga[place] = jnp.sum(gz[...], axis=0)
 
     def gs_gather(i):
-        peer = (t + 1 + i) % 32
-        return remote(ga.at[t], ga.at[t], ga_sem.at[0], ga_sem.at[1], tile=peer)
-
-    def go_gs_gather(i, carry):
-        gs_gather(i).start()
-        return carry
-
-    lax.fori_loop(0, 31, go_gs_gather, 0)
+        return remote(ga.at[place], ga.at[place], ga_sem.at[0], ga_sem.at[1], **plane_peer(i)[1])
+
+    loop(31, lambda i: gs_gather(i).start())
+    sent.append(lambda: drain(ga.at[pl.ds(0, 31)], ga_sem.at[0]))
     drain(ga.at[pl.ds(0, 31)], ga_sem.at[1])
-    gs_ref[...] = ga[...]
-
-    @pl.when(z % 4 == dy)
-    def _():
-        def done(i, carry):
-            w1_first(i).wait_send()
-            return carry
-
-        lax.fori_loop(0, 15, done, 0)
-
-    drain(tiles_hbm.at[pl.ds(0, 240)], w1_sem.at[2])
-    drain(red_in.at[pl.ds(0, 120)], red_sem.at[0])
-    drain(own_half.at[pl.ds(0, 120)], all_sem.at[0])
-    drain(msg.at[pl.ds(0, 15)], msg_sem.at[0])
-    drain(gs_in.at[pl.ds(0, 31)], gs_sem.at[0])
-    drain(gd.at[pl.ds(0, 15)], gd_sem.at[0])
-    drain(ga.at[pl.ds(0, 31)], ga_sem.at[0])
+    for k in range(8):
+        for j in range(4):
+            gs_ref[k : k + 1, 128 * j : 128 * j + 128] = ga[4 * k + j]
+
+    finish()
 
 
 def body(tiles, slide_of_tile, labels, attn_v, attn_u, score_w, head_w1, head_w2):
     rows, width = tiles.shape
     hid = attn_v.shape[1]
-    vmem, hbm = pl.BlockSpec(memory_space=pltpu.VMEM), pl.BlockSpec(memory_space=pl.ANY)
+    vmem, hbm = pl.BlockSpec(memory_space=pltpu.VMEM), pl.BlockSpec(memory_space=pltpu.HBM)
     dma = pltpu.SemaphoreType.DMA
     grad_w1, grad_score, grad_w2, loss = pl.pallas_call(
         kernel,
         out_shape=(
             jax.ShapeDtypeStruct((48, hid), f32),
-            jax.ShapeDtypeStruct((32, 1, 128), f32),
+            jax.ShapeDtypeStruct((8, hid), f32),
             jax.ShapeDtypeStruct((1, hid), f32),
             jax.ShapeDtypeStruct((1, 1), f32),
         ),
-        in_specs=[hbm, vmem, vmem, hbm, hbm, vmem, hbm, vmem],
+        in_specs=[hbm] * 8,
         out_specs=(vmem, vmem, vmem, vmem),
         scratch_shapes=[
             pltpu.VMEM((rows, width), bf16),
+            pltpu.VMEM((1, rows), jnp.int32),
+            pltpu.VMEM((1, 16), jnp.int32),
             pltpu.VMEM((width, hid), bf16),
             pltpu.VMEM((width, hid), bf16),
+            pltpu.VMEM((8, hid), bf16),
+            pltpu.VMEM((hid,), bf16),
             pltpu.VMEM((rows, hid), bf16),
             pltpu.VMEM((8, rows), f32),
             pltpu.VMEM((128, rows), f32),
@@ -428,13 +433,13 @@
             pltpu.VMEM((32, 1, 128), f32),
             pltpu.VMEM((16, 1, 128), f32),
             pltpu.VMEM((32, 1, 128), f32),
-            dma((8,)), dma((6,)), dma((4,)), dma((2,)), dma((2,)), dma((2,)), dma((2,)), dma((2,)), dma((2,)),
+            dma((12,)), dma((6,)), dma((4,)), dma((2,)), dma((2,)), dma((2,)), dma((2,)), dma((2,)), dma((2,)),
         ],
         compiler_params=pltpu.CompilerParams(
-            collective_id=0, has_side_effects=True, vmem_limit_bytes=48 * 1024 * 1024
+            collective_id=0, has_side_effects=True, vmem_limit_bytes=60 * 1024 * 1024
         ),
-    )(tiles, slide_of_tile, labels, attn_v, attn_u, score_w.T, head_w1, head_w2.reshape(1, hid))
-    return grad_w1, grad_score.reshape(8, hid).T, grad_w2.reshape(hid), loss.reshape(())
+    )(tiles, slide_of_tile, labels, attn_v, attn_u, score_w.T, head_w1, head_w2)
+    return grad_w1, grad_score.T, grad_w2.reshape(hid), loss.reshape(())
 
 
 def solution(mesh):

time: 84.2 us -> 70 us (0.83)
  Pallas kernels: 72.1 us -> 63.2 us
  local copies, waits for them, and re-layouts: 8.67 us -> 4.11 us
    pallas_call x1, Pallas kernels: 72.1 us -> 63.2 us  [body(): pl.pallas_call(kernel, out_shape=(jax.ShapeDtypeStruct((48, hid), f32), j...]
    unnamed x14 -> x3, local copies, waits for them, and re-layouts: 6.87 us -> 4.11 us
    reshape x2 -> x0, local copies, waits for them, and re-layouts: 1.29 us -> none  [the longest x1 0.68 us: body(): head_w2.reshape(1, hid)]
where the time goes in v2:
time: 70 us; the launch traced here: 69.7 us
  Pallas kernels  63.2 us (90%)
  local copies, waits for them, and re-layouts  4.11 us (6%)
  between operations  2.45 us (4%)
    pallas_call x1, Pallas kernels, body(): pl.pallas_call(kernel, out_shape=(jax.ShapeDtypeStruct((48, hid), f32), j...  63.2 us
    unnamed x3, local copies, waits for them, and re-layouts  4.11 us

profile of v2, /device:TPU:1, one launch (start us, length us, event | category | flops | bytes accessed | tf_op | source)
XLA Modules:
  0.0 69.7 jit_solution(16508063484954045936)
XLA Ops:
  0.6 63.2 %shard_map.111 = (f32[48,512]{1,0:T(8,128)}, f32[8,512]{1,0:T(8,128)}, f32[1,512]{1,0:T(1,128)}, f32[1,1]{1,0:T(1,128)}) custom-call(bf16[1024,1536]{1,0:T(8,128)(2,1)} %tiles_hbm.1, s32[1,1024]{1,0:T(1,128)} %seg_hbm.1, s32[1,16]{1,0:T(1,128)} %lab_hbm.1, bf16[1536,512]{1,0:T(8,128)(2,1)} %v_hbm.1, bf16[1536,512]{1,0:T(8,128)(2,1)} %u_hbm.1, ...), custom_call_target="tpu_custom_call" | custom-call | tf_op jit(solution)/shard_map/pallas_call | solution.py:401
  63.8 1.5 %copy.16 = f32[48,512]{1,0:T(8,128)} copy(f32[48,512]{1,0:T(8,128)} %get-tuple-element.16) | data formatting | bytes 196608
  65.3 1.3 %copy.17 = f32[512,8]{0,1:T(8,128)} copy(f32[512,8]{0,1:T(8,128)} %bitcast.4) | data formatting | bytes 32768
  66.7 1.2 %copy.18 = f32[512]{0:T(512)} copy(f32[512]{0:T(512)} %bitcast.6) | data formatting | bytes 4096

commit v3 on v2

--- a/solution.py
+++ b/solution.py
@@ -71,17 +71,25 @@
 
     place = 2 * d + c
 
+    def turn(i):
+        return 2 + 3 * i + 3 * (i * (i - 1) // 2)
+
+    def dp_peer(i):
+        return {"dp": (dx + turn(i // 4)) % 4 * 4 + (dy + turn(i % 4)) % 4}
+
     def plane_peer(i):
-        p = (place + 1 + i) % 32
-        return p, {"dp": p // 2, "tile": 2 * z + p % 2}
+        return {**dp_peer(i // 2), "tile": 2 * z + (c + 1 + i) % 2}
+
+    def z_place(i):
+        return (z + 8 + (1 - 2 * (i % 2)) * ((i + 1) // 2)) % 16
 
     def z_peer(i):
-        return {"tile": 2 * ((z + 1 + i) % 16) + c}
+        return {"tile": 2 * z_place(i) + c}
 
     def greet(who):
         pl.semaphore_signal(barrier, inc=1, device_id=who, device_id_type=MESH)
 
-    loop(31, lambda i: greet(plane_peer(i)[1]))
+    loop(31, lambda i: greet(plane_peer(i)))
     loop(15, lambda i: greet(z_peer(i)))
 
     loads = [
@@ -106,15 +114,14 @@
 
 
     def w1_first(i):
-        peer = (z + 1 + i) % 16
         return remote(
             w1_hbm.at[:, pl.ds(pl.multiple_of(dx * 128, 128), 128)],
-            w1.at[dx, z // 4, z % 4, c], w1_sem.at[0], w1_sem.at[1], tile=2 * peer + c,
+            w1.at[dx, z // 4, z % 4, c], w1_sem.at[0], w1_sem.at[1], **z_peer(i),
         )
 
     def w1_second(i):
         part = w1.at[dx, :, dy, c]
-        return remote(part, part, w1_sem.at[2], w1_sem.at[3], dp=(d + 1 + i) % 16)
+        return remote(part, part, w1_sem.at[2], w1_sem.at[3], **dp_peer(i))
 
     w1_third = remote(w1.at[:, :, :, c], w1.at[:, :, :, c], w1_sem.at[4], w1_sem.at[5], tile=other_t)
 
@@ -165,10 +172,11 @@
         scores[:, part] = matmul(sw[...], low, NT)
 
     for b in range(rows // BLOCK):
+        if b == 2:
+            pl.semaphore_wait(barrier, 46)
+            w1_start()
         loads[2 + b].wait()
         scorer(b)
-    pl.semaphore_wait(barrier, 46)
-    w1_start()
     for load in small[1:]:
         load.wait()
 
@@ -236,8 +244,7 @@
         return pl.ds(pl.multiple_of(8 * i, 8), 8)
 
     def reduce_copy(i):
-        peer = (z + 1 + i) % 16
-        return remote(red_out.at[eight(peer)], red_in.at[eight(z)], red_sem.at[0], red_sem.at[1], tile=2 * peer + c)
+        return remote(red_out.at[eight(z_place(i))], red_in.at[eight(z)], red_sem.at[0], red_sem.at[1], **z_peer(i))
 
     loop(15, lambda i: reduce_copy(i).start())
     sent.append(lambda: drain(red_in.at[pl.ds(0, 120)], red_sem.at[0]))
@@ -258,8 +265,7 @@
     own_half[eight(z), :] = jnp.concatenate(tile_rows + [slide_total, slide_top], axis=0)
 
     def gather_copy(i):
-        peer = (z + 1 + i) % 16
-        return remote(own_half.at[eight(z)], own_half.at[eight(z)], all_sem.at[0], all_sem.at[1], tile=2 * peer + c)
+        return remote(own_half.at[eight(z)], own_half.at[eight(z)], all_sem.at[0], all_sem.at[1], **z_peer(i))
 
     loop(15, lambda i: gather_copy(i).start())
     sent.append(lambda: drain(own_half.at[pl.ds(0, 120)], all_sem.at[0]))
@@ -315,7 +321,7 @@
     msg[d] = jnp.concatenate([pre_grad, normed_own, extra], axis=1).astype(bf16)
 
     def message(i):
-        return remote(msg.at[d], msg.at[d], msg_sem.at[0], msg_sem.at[1], dp=(d + 1 + i) % 16)
+        return remote(msg.at[d], msg.at[d], msg_sem.at[0], msg_sem.at[1], **dp_peer(i))
 
     loop(15, lambda i: message(i).start())
     sent.append(lambda: drain(msg.at[pl.ds(0, 15)], msg_sem.at[0]))
@@ -348,19 +354,15 @@
     both = matmul(jnp.concatenate([upper, lower], axis=0), gated[...])
     score_part = both[:8] + both[8:]
 
-    for k in range(8):
-        for j in range(4):
-            gs_out[4 * k + j] = score_part[k : k + 1, 128 * j : 128 * j + 128]
-
-    def gs_plane(i):
-        p, who = plane_peer(i)
-        return remote(gs_out.at[p], gs_in.at[place], gs_sem.at[0], gs_sem.at[1], **who)
-
-    loop(31, lambda i: gs_plane(i).start())
-    sent.append(lambda: drain(gs_in.at[pl.ds(0, 31)], gs_sem.at[0]))
-    gs_in[place] = gs_out[place]
-    drain(gs_in.at[pl.ds(0, 31)], gs_sem.at[1])
-    gz[z] = jnp.sum(gs_in[...], axis=0)
+    part, rest = score_part[:, :256], score_part[:, 256:]
+    gs_out[...] = pick(rest, part)
+    gs_swap = remote(gs_out, gs_in, gs_sem.at[0], gs_sem.at[1], tile=other_t)
+    gs_swap.start()
+    part = pick(part, rest)
+    gs_swap.wait()
+    part = part + gs_in[...]
+
+    gz[z] = jnp.concatenate([part[:, :128], part[:, 128:]], axis=0).astype(bf16)
 
     def gs_z(i):
         return remote(gz.at[z], gz.at[z], gz_sem.at[0], gz_sem.at[1], **z_peer(i))
@@ -378,19 +380,31 @@
     loss_ref[...] = sums[4:5, 0:1] * (1.0 / 256.0)
 
     drain(gz.at[pl.ds(0, 15)], gz_sem.at[1])
-    ga[place] = jnp.sum(gz[...], axis=0)
-
-    def gs_gather(i):
-        return remote(ga.at[place], ga.at[place], ga_sem.at[0], ga_sem.at[1], **plane_peer(i)[1])
-
-    loop(31, lambda i: gs_gather(i).start())
+
+    ga[place] = jnp.sum(gz[...].astype(f32), axis=0).astype(bf16)
+
+    def gs_plane(i):
+        return remote(ga.at[place], ga.at[place], ga_sem.at[0], ga_sem.at[1], **plane_peer(i))
+
+    loop(31, lambda i: gs_plane(i).start())
     sent.append(lambda: drain(ga.at[pl.ds(0, 31)], ga_sem.at[0]))
     drain(ga.at[pl.ds(0, 31)], ga_sem.at[1])
-    for k in range(8):
-        for j in range(4):
-            gs_ref[k : k + 1, 128 * j : 128 * j + 128] = ga[4 * k + j]
+    parts = ga[...].astype(f32).reshape(16, 2, 16, 128)
+    for half in range(2):
+        sums = jnp.sum(parts[:, half], axis=0)
+        gs_ref[:, 256 * half : 256 * half + 128] = sums[:8]
+        gs_ref[:, 256 * half + 128 : 256 * half + 256] = sums[8:]
 
     finish()
+
+
+def publish(*refs):
+    sems = refs[8]
+    copies = [pltpu.make_async_copy(refs[i], refs[4 + i], sems.at[i]) for i in range(4)]
+    for copy in copies:
+        copy.start()
+    for copy in copies:
+        copy.wait()
 
 
 def body(tiles, slide_of_tile, labels, attn_v, attn_u, score_w, head_w1, head_w2):
@@ -398,14 +412,10 @@
     hid = attn_v.shape[1]
     vmem, hbm = pl.BlockSpec(memory_space=pltpu.VMEM), pl.BlockSpec(memory_space=pltpu.HBM)
     dma = pltpu.SemaphoreType.DMA
-    grad_w1, grad_score, grad_w2, loss = pl.pallas_call(
+    shapes = tuple(jax.ShapeDtypeStruct(shape, f32) for shape in ((48, hid), (8, hid), (1, hid), (1, 1)))
+    results = pl.pallas_call(
         kernel,
-        out_shape=(
-            jax.ShapeDtypeStruct((48, hid), f32),
-            jax.ShapeDtypeStruct((8, hid), f32),
-            jax.ShapeDtypeStruct((1, hid), f32),
-            jax.ShapeDtypeStruct((1, 1), f32),
-        ),
+        out_shape=shapes,
         in_specs=[hbm] * 8,
         out_specs=(vmem, vmem, vmem, vmem),
         scratch_shapes=[
@@ -429,16 +439,19 @@
             pltpu.VMEM((128, 128), f32),
             pltpu.VMEM((16, width + 128), f32),
             pltpu.VMEM((16, 16, 768), bf16),
-            pltpu.VMEM((32, 1, 128), f32),
-            pltpu.VMEM((32, 1, 128), f32),
-            pltpu.VMEM((16, 1, 128), f32),
-            pltpu.VMEM((32, 1, 128), f32),
+            pltpu.VMEM((8, 256), f32),
+            pltpu.VMEM((8, 256), f32),
+            pltpu.VMEM((16, 16, 128), bf16),
+            pltpu.VMEM((32, 16, 128), bf16),
             dma((12,)), dma((6,)), dma((4,)), dma((2,)), dma((2,)), dma((2,)), dma((2,)), dma((2,)), dma((2,)),
         ],
         compiler_params=pltpu.CompilerParams(
             collective_id=0, has_side_effects=True, vmem_limit_bytes=60 * 1024 * 1024
         ),
     )(tiles, slide_of_tile, labels, attn_v, attn_u, score_w.T, head_w1, head_w2)
+    grad_w1, grad_score, grad_w2, loss = pl.pallas_call(
+        publish, out_shape=shapes, in_specs=[hbm] * 4, out_specs=(hbm,) * 4, scratch_shapes=[dma((4,))]
+    )(*results)
     return grad_w1, grad_score.T, grad_w2.reshape(hid), loss.reshape(())
 
 

time: 70 us -> 63.5 us (0.907)
  local copies, waits for them, and re-layouts: 4.11 us -> 0 us
  between operations: 2.45 us -> 0.64 us
    unnamed x3 -> x0, local copies, waits for them, and re-layouts: 4.11 us -> none
    pallas_call x1 -> x2, Pallas kernels: 63.2 us -> 62.7 us  [the longest x1 57.4 us: body(): pl.pallas_call(kernel, out_shape=shapes, in_specs=[hbm] * 8, out_specs=(v...]
where the time goes in v3:
time: 63.5 us; the launch traced here: 63.4 us
  Pallas kernels  62.7 us (99%)
  between operations  0.64 us (1%)
    pallas_call x1, Pallas kernels, body(): pl.pallas_call(kernel, out_shape=shapes, in_specs=[hbm] * 8, out_specs=(v...  57.4 us
    pallas_call x1, Pallas kernels, body(): pl.pallas_call(publish, out_shape=shapes, in_specs=[hbm] * 4, out_specs=(...  5.3 us

profile of v3, /device:TPU:1, one launch (start us, length us, event | category | flops | bytes accessed | tf_op | source)
XLA Modules:
  0.0 63.4 jit_solution(83520933553756943)
XLA Ops:
  0.6 57.4 %shard_map.111 = (f32[48,512]{1,0:T(8,128)}, f32[8,512]{1,0:T(8,128)}, f32[1,512]{1,0:T(1,128)}, f32[1,1]{1,0:T(1,128)}) custom-call(bf16[1024,1536]{1,0:T(8,128)(2,1)} %tiles_hbm.1, s32[1,1024]{1,0:T(1,128)} %seg_hbm.1, s32[1,16]{1,0:T(1,128)} %lab_hbm.1, bf16[1536,512]{1,0:T(8,128)(2,1)} %v_hbm.1, bf16[1536,512]{1,0:T(8,128)(2,1)} %u_hbm.1, ...), custom_call_target="tpu_custom_call" | custom-call | tf_op jit(solution)/shard_map/pallas_call | solution.py:416
  58.1 5.3 %shard_map.112 = (f32[48,512]{1,0:T(8,128)}, f32[8,512]{1,0:T(8,128)}, f32[1,512]{1,0:T(1,128)}, f32[1,1]{1,0:T(1,128)}) custom-call(f32[48,512]{1,0:T(8,128)} %get-tuple-element.12.refs_0_, f32[8,512]{1,0:T(8,128)} %get-tuple-element.13.refs_1_, f32[1,512]{1,0:T(1,128)} %get-tuple-element.14.refs_2_, f32[1,1]{1,0:T(1,128)} %get-tuple-element.15.refs_3_), custom_call_target="tpu_custom_call" | custom-call | tf_op jit(solution)/shard_map/pallas_call | solution.py:452

commit v4 on v3

--- a/solution.py
+++ b/solution.py
@@ -85,12 +85,6 @@
 
     def z_peer(i):
         return {"tile": 2 * z_place(i) + c}
-
-    def greet(who):
-        pl.semaphore_signal(barrier, inc=1, device_id=who, device_id_type=MESH)
-
-    loop(31, lambda i: greet(plane_peer(i)))
-    loop(15, lambda i: greet(z_peer(i)))
 
     loads = [
         pltpu.make_async_copy(v_hbm, wv, load_sem.at[0]),
@@ -109,8 +103,14 @@
         w1_hbm.at[:, pl.ds(pl.multiple_of(dx * 128, 128), 128)],
         w1.at[dx, z // 4, z % 4, c], load_sem.at[7],
     )
-    for load in loads + small:
+    for load in [loads[2], *loads[:2], small[0], *loads[3:], *small[1:]]:
         load.start()
+
+    def greet(who):
+        pl.semaphore_signal(barrier, inc=1, device_id=who, device_id_type=MESH)
+
+    loop(31, lambda i: greet(plane_peer(i)))
+    loop(15, lambda i: greet(z_peer(i)))
 
 
     def w1_first(i):
@@ -158,14 +158,15 @@
     def w1_end():
         w1_third.wait()
 
-    loads[0].wait()
-    loads[1].wait()
-    small[0].wait()
-
     def scorer(b):
         part = pl.ds(b * BLOCK, BLOCK)
         x = tiles[part, :]
+        if b == 0:
+            loads[0].wait()
         tanh_part = jnp.tanh(matmul(x, wv[...]))
+        if b == 0:
+            loads[1].wait()
+            small[0].wait()
         gate_part = 0.5 + 0.5 * jnp.tanh(0.5 * matmul(x, wu[...]))
         low = (tanh_part * gate_part).astype(bf16)
         gated[part, :] = low
@@ -303,29 +304,6 @@
     w2_part = jnp.sum(logit_grad * hidden, axis=0, keepdims=True)
     pre_grad = logit_grad * w2_float * gelu_slope(pre_act, phi)
 
-    wide[:, :width] = normed_low.astype(f32)
-    wide[:, width:] = jnp.zeros((16, 128), f32)
-    first = 48 * t
-    window = wide[:, pl.ds(pl.multiple_of(first // 128 * 128, 128), 256)].astype(bf16)
-    chosen = lax.broadcasted_iota(jnp.int32, (256, 128), 0) == (
-        lax.broadcasted_iota(jnp.int32, (256, 128), 1) + first % 128
-    )
-    normed_own = matmul(window, jnp.where(chosen, 1.0, 0.0).astype(bf16))
-    sub = lax.broadcasted_iota(jnp.int32, (16, 128), 0)
-    extra = jnp.zeros((16, 128), f32)
-    for j in range(5):
-        piece = w2_part[:, 128 * j : 128 * j + 128] if j < 4 else jnp.broadcast_to(loss_part, (1, 128))
-        upper = piece.astype(bf16).astype(f32)
-        extra = jnp.where(sub == j, upper, extra)
-        extra = jnp.where(sub == 8 + j, piece - upper, extra)
-    msg[d] = jnp.concatenate([pre_grad, normed_own, extra], axis=1).astype(bf16)
-
-    def message(i):
-        return remote(msg.at[d], msg.at[d], msg_sem.at[0], msg_sem.at[1], **dp_peer(i))
-
-    loop(15, lambda i: message(i).start())
-    sent.append(lambda: drain(msg.at[pl.ds(0, 15)], msg_sem.at[0]))
-
     upper, lower = split(pre_grad)
     both = matmul(jnp.concatenate([upper, lower], axis=0), whole, NT)
     norm_grad = both[:16] + both[16:]
@@ -359,6 +337,29 @@
     gs_swap = remote(gs_out, gs_in, gs_sem.at[0], gs_sem.at[1], tile=other_t)
     gs_swap.start()
     part = pick(part, rest)
+
+    wide[:, :width] = normed_low.astype(f32)
+    wide[:, width:] = jnp.zeros((16, 128), f32)
+    first = 48 * t
+    window = wide[:, pl.ds(pl.multiple_of(first // 128 * 128, 128), 256)].astype(bf16)
+    chosen = lax.broadcasted_iota(jnp.int32, (256, 128), 0) == (
+        lax.broadcasted_iota(jnp.int32, (256, 128), 1) + first % 128
+    )
+    normed_own = matmul(window, jnp.where(chosen, 1.0, 0.0).astype(bf16))
+    sub = lax.broadcasted_iota(jnp.int32, (16, 128), 0)
+    extra = jnp.zeros((16, 128), f32)
+    for j in range(5):
+        piece = w2_part[:, 128 * j : 128 * j + 128] if j < 4 else jnp.broadcast_to(loss_part, (1, 128))
+        upper = piece.astype(bf16).astype(f32)
+        extra = jnp.where(sub == j, upper, extra)
+        extra = jnp.where(sub == 8 + j, piece - upper, extra)
+    msg[d] = jnp.concatenate([pre_grad, normed_own, extra], axis=1).astype(bf16)
+
+    def message(i):
+        return remote(msg.at[d], msg.at[d], msg_sem.at[0], msg_sem.at[1], **dp_peer(i))
+
+    loop(15, lambda i: message(i).start())
+    sent.append(lambda: drain(msg.at[pl.ds(0, 15)], msg_sem.at[0]))
     gs_swap.wait()
     part = part + gs_in[...]
 
@@ -370,6 +371,15 @@
     loop(15, lambda i: gs_z(i).start())
     sent.append(lambda: drain(gz.at[pl.ds(0, 15)], gz_sem.at[0]))
 
+    drain(gz.at[pl.ds(0, 15)], gz_sem.at[1])
+
+    ga[place] = jnp.sum(gz[...].astype(f32), axis=0).astype(bf16)
+
+    def gs_plane(i):
+        return remote(ga.at[place], ga.at[place], ga_sem.at[0], ga_sem.at[1], **plane_peer(i))
+
+    loop(31, lambda i: gs_plane(i).start())
+    sent.append(lambda: drain(ga.at[pl.ds(0, 31)], ga_sem.at[0]))
     drain(msg.at[pl.ds(0, 15)], msg_sem.at[1])
     grads = msg[:, :, 0:512].reshape(256, 512)
     own = msg[:, :, 512:640].reshape(256, 128)
@@ -379,15 +389,6 @@
     gw2_ref[...] = jnp.concatenate([sums[j : j + 1] for j in range(4)], axis=1)
     loss_ref[...] = sums[4:5, 0:1] * (1.0 / 256.0)
 
-    drain(gz.at[pl.ds(0, 15)], gz_sem.at[1])
-
-    ga[place] = jnp.sum(gz[...].astype(f32), axis=0).astype(bf16)
-
-    def gs_plane(i):
-        return remote(ga.at[place], ga.at[place], ga_sem.at[0], ga_sem.at[1], **plane_peer(i))
-
-    loop(31, lambda i: gs_plane(i).start())
-    sent.append(lambda: drain(ga.at[pl.ds(0, 31)], ga_sem.at[0]))
     drain(ga.at[pl.ds(0, 31)], ga_sem.at[1])
     parts = ga[...].astype(f32).reshape(16, 2, 16, 128)
     for half in range(2):
@@ -396,15 +397,6 @@
         gs_ref[:, 256 * half + 128 : 256 * half + 256] = sums[8:]
 
     finish()
-
-
-def publish(*refs):
-    sems = refs[8]
-    copies = [pltpu.make_async_copy(refs[i], refs[4 + i], sems.at[i]) for i in range(4)]
-    for copy in copies:
-        copy.start()
-    for copy in copies:
-        copy.wait()
 
 
 def body(tiles, slide_of_tile, labels, attn_v, attn_u, score_w, head_w1, head_w2):
@@ -415,7 +407,7 @@
     shapes = tuple(jax.ShapeDtypeStruct(shape, f32) for shape in ((48, hid), (8, hid), (1, hid), (1, 1)))
     results = pl.pallas_call(
         kernel,
-        out_shape=shapes,
+        out_shape=tuple(pltpu.VMEM(x.shape, f32) for x in shapes),
         in_specs=[hbm] * 8,
         out_specs=(vmem, vmem, vmem, vmem),
         scratch_shapes=[
@@ -449,9 +441,7 @@
             collective_id=0, has_side_effects=True, vmem_limit_bytes=60 * 1024 * 1024
         ),
     )(tiles, slide_of_tile, labels, attn_v, attn_u, score_w.T, head_w1, head_w2)
-    grad_w1, grad_score, grad_w2, loss = pl.pallas_call(
-        publish, out_shape=shapes, in_specs=[hbm] * 4, out_specs=(hbm,) * 4, scratch_shapes=[dma((4,))]
-    )(*results)
+    grad_w1, grad_score, grad_w2, loss = results
     return grad_w1, grad_score.T, grad_w2.reshape(hid), loss.reshape(())
 
 

time: 63.5 us -> 58.1 us (0.915)
  Pallas kernels: 62.7 us -> 54.3 us
  local copies, waits for them, and re-layouts: 0 us -> 1.83 us
  between operations: 0.64 us -> 1.81 us
    pallas_call x2 -> x1, Pallas kernels: 62.7 us -> 54.3 us  [body(): pl.pallas_call(kernel, out_shape=tuple((pltpu.VMEM(x.shape, f32) for x in...]
    unnamed x0 -> x3, local copies, waits for them, and re-layouts: none -> 1.83 us
where the time goes in v4:
time: 58.1 us; the launch traced here: 58 us
  Pallas kernels  54.3 us (93%)
  local copies, waits for them, and re-layouts  1.83 us (3%)
  between operations  1.81 us (3%)
    pallas_call x1, Pallas kernels, body(): pl.pallas_call(kernel, out_shape=tuple((pltpu.VMEM(x.shape, f32) for x in...  54.3 us
    unnamed x3, local copies, waits for them, and re-layouts  1.83 us

profile of v4, /device:TPU:1, one launch (start us, length us, event | category | flops | bytes accessed | tf_op | source)
XLA Modules:
  0.0 58.0 jit_solution(14007637449684313110)
XLA Ops:
  0.6 54.3 %shard_map.111 = (f32[48,512]{1,0:T(8,128)S(1)}, f32[8,512]{1,0:T(8,128)S(1)}, f32[1,512]{1,0:T(1,128)S(1)}, f32[1,1]{1,0:T(1,128)S(1)}) custom-call(bf16[1024,1536]{1,0:T(8,128)(2,1)} %tiles_hbm.1, s32[1,1024]{1,0:T(1,128)} %seg_hbm.1, s32[1,16]{1,0:T(1,128)} %lab_hbm.1, bf16[1536,512]{1,0:T(8,128)(2,1)} %v_hbm.1, bf16[1536,512]{1,0:T(8,128)(2,1)} %u_hbm.1, ...), custom_call_target="tpu_custom_call" | custom-call | tf_op jit(solution)/shard_map/pallas_call | solution.py:408
  55.0 0.6 %copy.16 = f32[48,512]{1,0:T(8,128)} copy(f32[48,512]{1,0:T(8,128)S(1)} %get-tuple-element.12) | data formatting | bytes 196608
  55.7 0.6 %copy.17 = f32[512,8]{0,1:T(8,128)} copy(f32[512,8]{0,1:T(8,128)S(1)} %bitcast.4) | data formatting | bytes 32768
  56.3 0.6 copy.18

commit v5 on v4

--- a/solution.py
+++ b/solution.py
@@ -85,6 +85,11 @@
 
     def z_peer(i):
         return {"tile": 2 * z_place(i) + c}
+
+    def greet(who):
+        pl.semaphore_signal(barrier, inc=1, device_id=who, device_id_type=MESH)
+
+    loop(15, lambda i: greet(z_peer(i)))
 
     loads = [
         pltpu.make_async_copy(v_hbm, wv, load_sem.at[0]),
@@ -106,11 +111,7 @@
     for load in [loads[2], *loads[:2], small[0], *loads[3:], *small[1:]]:
         load.start()
 
-    def greet(who):
-        pl.semaphore_signal(barrier, inc=1, device_id=who, device_id_type=MESH)
-
     loop(31, lambda i: greet(plane_peer(i)))
-    loop(15, lambda i: greet(z_peer(i)))
 
 
     def w1_first(i):

time: 58.1 us -> 57.1 us (0.983)
  Pallas kernels: 54.3 us -> 53.3 us
    pallas_call x1, Pallas kernels: 54.3 us -> 53.3 us  [body(): pl.pallas_call(kernel, out_shape=tuple((pltpu.VMEM(x.shape, f32) for x in...]
where the time goes in v5:
time: 57.1 us; the launch traced here: 56.9 us
  Pallas kernels  53.3 us (93%)
  local copies, waits for them, and re-layouts  1.83 us (3%)
  between operations  1.81 us (3%)
    pallas_call x1, Pallas kernels, body(): pl.pallas_call(kernel, out_shape=tuple((pltpu.VMEM(x.shape, f32) for x in...  53.3 us
    unnamed x3, local copies, waits for them, and re-layouts  1.83 us

profile of v5, /device:TPU:1, one launch (start us, length us, event | category | flops | bytes accessed | tf_op | source)
XLA Modules:
  0.0 56.9 jit_solution(8438315436757647734)
XLA Ops:
  0.6 53.3 %shard_map.111 = (f32[48,512]{1,0:T(8,128)S(1)}, f32[8,512]{1,0:T(8,128)S(1)}, f32[1,512]{1,0:T(1,128)S(1)}, f32[1,1]{1,0:T(1,128)S(1)}) custom-call(bf16[1024,1536]{1,0:T(8,128)(2,1)} %tiles_hbm.1, s32[1,1024]{1,0:T(1,128)} %seg_hbm.1, s32[1,16]{1,0:T(1,128)} %lab_hbm.1, bf16[1536,512]{1,0:T(8,128)(2,1)} %v_hbm.1, bf16[1536,512]{1,0:T(8,128)(2,1)} %u_hbm.1, ...), custom_call_target="tpu_custom_call" | custom-call | tf_op jit(solution)/shard_map/pallas_call | solution.py:409
  54.0 0.6 %copy.16 = f32[48,512]{1,0:T(8,128)} copy(f32[48,512]{1,0:T(8,128)S(1)} %get-tuple-element.12) | data formatting | bytes 196608
  54.6 0.6 %copy.17 = f32[512,8]{0,1:T(8,128)} copy(f32[512,8]{0,1:T(8,128)S(1)} %bitcast.4) | data formatting | bytes 32768
  55.2 0.6 %copy.18 = f32[512]{0:T(512)} copy(f32[512]{0:T(512)S(1)} %bitcast.5) | data formatting | bytes 4096

commit v6 on v5

--- a/solution.py
+++ b/solution.py
@@ -194,17 +194,20 @@
         top = jnp.where(lane == k, peak, top)
         total = jnp.where(lane == k, jnp.sum(term, axis=1, keepdims=True), total)
 
-    blocks = []
-    for q in range(4):
-        upper, lower = split(expo[32 * q : 32 * q + 32, :])
-        both = matmul(jnp.concatenate([upper, lower], axis=0), tiles[:, 384 * q : 384 * q + 384])
-        both = both[:32] + both[32:]
-        first, second = both[:16], both[16:]
-        blocks += [
-            first[:, :128],
-            jnp.where(lane < 64, first[:, 128:256], second[:, 128:256]),
-            second[:, 256:],
-        ]
+    def pool(half):
+        blocks = []
+        for i in range(2):
+            upper, lower = split(expo[pl.ds(pl.multiple_of(64 * half + 32 * i, 32), 32), :])
+            part = tiles[:, pl.ds(pl.multiple_of(768 * half + 384 * i, 128), 384)]
+            both = matmul(jnp.concatenate([upper, lower], axis=0), part)
+            both = both[:32] + both[32:]
+            first, second = both[:16], both[16:]
+            blocks += [
+                first[:, :128],
+                jnp.where(lane < 64, first[:, 128:256], second[:, 128:256]),
+                second[:, 256:],
+            ]
+        return blocks
 
     def pick(a, b):
         return jnp.where(c == 0, a, b)
@@ -212,13 +215,13 @@
     def strided(j):
         return pl.ds(j, 16, stride=8)
 
-    for j in range(6):
-        swap_out[strided(j), :] = pick(blocks[6 + j], blocks[j])
+    for j, block in enumerate(pool(1 - c)):
+        swap_out[strided(j), :] = block
     swap_out[strided(6), :] = total
     swap_out[strided(7), :] = top
     swap = remote(swap_out, swap_in, half_sem.at[0], half_sem.at[1], tile=other_t)
     swap.start()
-    mine = [pick(blocks[j], blocks[6 + j]) for j in range(6)]
+    mine = pool(c)
     swap.wait()
 
     low_lane = lane < 64
@@ -330,14 +333,26 @@
             delta[k : k + 1, :] = jnp.sum(change, axis=0, keepdims=True)
 
     upper, lower = split(delta[...])
-    both = matmul(jnp.concatenate([upper, lower], axis=0), gated[...])
-    score_part = both[:8] + both[8:]
-
-    part, rest = score_part[:, :256], score_part[:, 256:]
-    gs_out[...] = pick(rest, part)
+    change = jnp.concatenate([upper, lower], axis=0)
+
+    def score_part(half):
+        both = matmul(change, gated[:, pl.ds(pl.multiple_of(256 * half, 256), 256)])
+        return both[:8] + both[8:]
+
+    gs_out[...] = score_part(1 - c)
     gs_swap = remote(gs_out, gs_in, gs_sem.at[0], gs_sem.at[1], tile=other_t)
     gs_swap.start()
-    part = pick(part, rest)
+    part = score_part(c)
+    gs_swap.wait()
+    part = part + gs_in[...]
+
+    gz[z] = jnp.concatenate([part[:, :128], part[:, 128:]], axis=0).astype(bf16)
+
+    def gs_z(i):
+        return remote(gz.at[z], gz.at[z], gz_sem.at[0], gz_sem.at[1], **z_peer(i))
+
+    loop(15, lambda i: gs_z(i).start())
+    sent.append(lambda: drain(gz.at[pl.ds(0, 15)], gz_sem.at[0]))
 
     wide[:, :width] = normed_low.astype(f32)
     wide[:, width:] = jnp.zeros((16, 128), f32)
@@ -361,16 +376,6 @@
 
     loop(15, lambda i: message(i).start())
     sent.append(lambda: drain(msg.at[pl.ds(0, 15)], msg_sem.at[0]))
-    gs_swap.wait()
-    part = part + gs_in[...]
-
-    gz[z] = jnp.concatenate([part[:, :128], part[:, 128:]], axis=0).astype(bf16)
-
-    def gs_z(i):
-        return remote(gz.at[z], gz.at[z], gz_sem.at[0], gz_sem.at[1], **z_peer(i))
-
-    loop(15, lambda i: gs_z(i).start())
-    sent.append(lambda: drain(gz.at[pl.ds(0, 15)], gz_sem.at[0]))
 
     drain(gz.at[pl.ds(0, 15)], gz_sem.at[1])
 

time: 57.1 us -> 56.9 us (level)
  no operation moved by 1% of the time
where the time goes in v6:
time: 56.9 us; the launch traced here: 56.7 us
  Pallas kernels  53.1 us (93%)
  local copies, waits for them, and re-layouts  1.83 us (3%)
  between operations  1.81 us (3%)
    pallas_call x1, Pallas kernels, body(): pl.pallas_call(kernel, out_shape=tuple((pltpu.VMEM(x.shape, f32) for x in...  53.1 us
    unnamed x3, local copies, waits for them, and re-layouts  1.83 us

profile of v6, /device:TPU:1, one launch (start us, length us, event | category | flops | bytes accessed | tf_op | source)
XLA Modules:
  0.0 56.7 jit_solution(14259371235159237788)
XLA Ops:
  0.6 53.1 %shard_map.111 = (f32[48,512]{1,0:T(8,128)S(1)}, f32[8,512]{1,0:T(8,128)S(1)}, f32[1,512]{1,0:T(1,128)S(1)}, f32[1,1]{1,0:T(1,128)S(1)}) custom-call(bf16[1024,1536]{1,0:T(8,128)(2,1)} %tiles_hbm.1, s32[1,1024]{1,0:T(1,128)} %seg_hbm.1, s32[1,16]{1,0:T(1,128)} %lab_hbm.1, bf16[1536,512]{1,0:T(8,128)(2,1)} %v_hbm.1, bf16[1536,512]{1,0:T(8,128)(2,1)} %u_hbm.1, ...), custom_call_target="tpu_custom_call" | custom-call | tf_op jit(solution)/shard_map/pallas_call | solution.py:414
  53.8 0.6 %copy.16 = f32[48,512]{1,0:T(8,128)} copy(f32[48,512]{1,0:T(8,128)S(1)} %get-tuple-element.12) | data formatting | bytes 196608
  54.4 0.6 %copy.17 = f32[512,8]{0,1:T(8,128)} copy(f32[512,8]{0,1:T(8,128)S(1)} %bitcast.4) | data formatting | bytes 32768
  55.0 0.6 %copy.18 = f32[512]{0:T(512)} copy(f32[512]{0:T(512)S(1)} %bitcast.5) | data formatting | bytes 4096

commit v7 on v6

--- a/solution.py
+++ b/solution.py
@@ -120,11 +120,13 @@
             w1.at[dx, z // 4, z % 4, c], w1_sem.at[0], w1_sem.at[1], **z_peer(i),
         )
 
-    def w1_second(i):
-        part = w1.at[dx, :, dy, c]
-        return remote(part, part, w1_sem.at[2], w1_sem.at[3], **dp_peer(i))
-
-    w1_third = remote(w1.at[:, :, :, c], w1.at[:, :, :, c], w1_sem.at[4], w1_sem.at[5], tile=other_t)
+    def w1_second(half, i):
+        part = w1.at[dx, pl.ds(2 * half, 2), dy, c]
+        return remote(part, part, w1_sem.at[2 + half], w1_sem.at[4 + half], **dp_peer(i))
+
+    def w1_third(half):
+        part = w1.at[:, pl.ds(2 * half, 2), :, c]
+        return remote(part, part, w1_sem.at[6 + half], w1_sem.at[8 + half], tile=other_t)
 
     def w1_start():
         @pl.when(z % 4 == dy)
@@ -149,15 +151,19 @@
         def _():
             drain(w1.at[0, :, 0, 0], w1_sem.at[1])
 
-        loop(15, lambda i: w1_second(i).start())
-        sent.append(lambda: drain(tiles_hbm.at[pl.ds(0, 240)], w1_sem.at[2]))
+        loop(15, lambda i: w1_second(0, i).start())
+        loop(15, lambda i: w1_second(1, i).start())
+        sent.append(lambda: drain(tiles_hbm.at[pl.ds(0, 120)], w1_sem.at[2]))
+        sent.append(lambda: drain(tiles_hbm.at[pl.ds(0, 120)], w1_sem.at[3]))
 
     def w1_last():
-        drain(tiles_hbm.at[pl.ds(0, 240)], w1_sem.at[3])
-        w1_third.start()
+        for half in range(2):
+            drain(tiles_hbm.at[pl.ds(0, 120)], w1_sem.at[4 + half])
+            w1_third(half).start()
 
     def w1_end():
-        w1_third.wait()
+        w1_third(0).wait()
+        w1_third(1).wait()
 
     def scorer(b):
         part = pl.ds(b * BLOCK, BLOCK)
@@ -441,7 +447,7 @@
             pltpu.VMEM((8, 256), f32),
             pltpu.VMEM((16, 16, 128), bf16),
             pltpu.VMEM((32, 16, 128), bf16),
-            dma((12,)), dma((6,)), dma((4,)), dma((2,)), dma((2,)), dma((2,)), dma((2,)), dma((2,)), dma((2,)),
+            dma((12,)), dma((10,)), dma((4,)), dma((2,)), dma((2,)), dma((2,)), dma((2,)), dma((2,)), dma((2,)),
         ],
         compiler_params=pltpu.CompilerParams(
             collective_id=0, has_side_effects=True, vmem_limit_bytes=60 * 1024 * 1024

time: 56.9 us -> 56.8 us (level)
  no operation moved by 1% of the time
where the time goes in v7:
time: 56.8 us; the launch traced here: 56.7 us
  Pallas kernels  53.1 us (93%)
  local copies, waits for them, and re-layouts  1.83 us (3%)
  between operations  1.81 us (3%)
    pallas_call x1, Pallas kernels, body(): pl.pallas_call(kernel, out_shape=tuple((pltpu.VMEM(x.shape, f32) for x in...  53.1 us
    unnamed x3, local copies, waits for them, and re-layouts  1.83 us

profile of v7, /device:TPU:1, one launch (start us, length us, event | category | flops | bytes accessed | tf_op | source)
XLA Modules:
  0.0 56.7 jit_solution(12202061278717569678)
XLA Ops:
  0.6 53.1 %shard_map.111 = (f32[48,512]{1,0:T(8,128)S(1)}, f32[8,512]{1,0:T(8,128)S(1)}, f32[1,512]{1,0:T(1,128)S(1)}, f32[1,1]{1,0:T(1,128)S(1)}) custom-call(bf16[1024,1536]{1,0:T(8,128)(2,1)} %tiles_hbm.1, s32[1,1024]{1,0:T(1,128)} %seg_hbm.1, s32[1,16]{1,0:T(1,128)} %lab_hbm.1, bf16[1536,512]{1,0:T(8,128)(2,1)} %v_hbm.1, bf16[1536,512]{1,0:T(8,128)(2,1)} %u_hbm.1, ...), custom_call_target="tpu_custom_call" | custom-call | tf_op jit(solution)/shard_map/pallas_call | solution.py:420
  53.7 0.6 %copy.16 = f32[48,512]{1,0:T(8,128)} copy(f32[48,512]{1,0:T(8,128)S(1)} %get-tuple-element.12) | data formatting | bytes 196608
  54.4 0.6 %copy.17 = f32[512,8]{0,1:T(8,128)} copy(f32[512,8]{0,1:T(8,128)S(1)} %bitcast.4) | data formatting | bytes 32768
  55.0 0.6 %copy.18 = f32[512]{0:T(512)} copy(f32[512]{0:T(512)S(1)} %bitcast.5) | data formatting | bytes 4096
